TPU v7x, 32 devices: a whole 2x2x4 slice. The times are simulated.
32 devices in a mesh: lst: 4 (over y, x), night: 8 (over z, core).
Axes of the slice: x: 2, y: 2, z: 4, core: 2. Of those that a mesh axis runs over, the one named last changes fastest.
Arguments:
- visibility: bfloat16 [8, 32, 16, 2, 1536], P('night', 'lst'), may hold values from -18 to 18
- flags: int32 [8, 32, 16, 1536], P('night', 'lst'), may hold values 0 or 1
- counts: int32 [8, 32], P('night', 'lst'), may hold values from 1 to 4
- offsets: int32 [8], P('night'), may hold values from -6 to 6, as said below
- fraction: float32 [8], P('night'), may hold values from 0 to 1
- gains: float32 [8, 2, 1536], P('night'), may hold values from -6 to 6
- inverse_var: float32 [8, 1536], P('night'), may hold values from 0.005 to 0.05
- prior: float32 [1536], replicated, may hold values from 0.5 to 5
Outputs:
- binned: bfloat16 [32, 16, 2, 1536], P('lst')
- weight_total: float32 [32, 16, 1536], P('lst')
Inputs may be any that keep to these rules, and one draw needn't show every extreme that they name: `offsets`: both -6 and 6 occur among the nights.
All inputs are finite; a program needn't handle non-finite values. No bound on the sum of `flags` on one device may be relied on, other than what follows from the above.
Results may differ from a plain program's by a relative error of at most 0.009.
Values may be sent and summed in bfloat16 or wider, within the bound.
A program may use at most 64 MiB of HBM per device.

v0:
```python
import jax
import jax.numpy as jnp
from jax import lax
from jax.sharding import PartitionSpec as P


def extended(x, sides, width):
    for axis, dim in sides:
        size, length = (lax.axis_size(axis), x.shape[dim])
        up = [(i, (i + 1) % size) for i in range(size)]
        down = [(j, i) for i, j in up]
        last = lax.slice_in_dim(x, length - width, length, axis=dim)
        first = lax.slice_in_dim(x, 0, width, axis=dim)
        before = lax.ppermute(last, axis, up)
        after = lax.ppermute(first, axis, down)
        x = jnp.concatenate([before, x, after], axis=dim)
    return x


def spline_taps(fraction):
    cube = fraction * fraction * fraction
    square = fraction * fraction
    first = (1.0 - fraction) ** 3 / 6.0
    second = (3.0 * cube - 6.0 * square + 4.0) / 6.0
    third = (-3.0 * cube + 3.0 * square + 3.0 * fraction + 1.0) / 6.0
    fourth = cube / 6.0
    return jnp.stack([first, second, third, fourth], axis=-1)


def shards(visibility, flags, counts, offsets, fraction, gains, inverse_var, prior):
    local_nights = visibility.shape[0]
    sample_count = visibility.shape[1]
    baseline_count = visibility.shape[2]
    channel_count = visibility.shape[4]
    scale = (flags * counts[:, :, None, None]).astype(jnp.float32) * inverse_var[:, None, None, :]
    weight = scale.astype(jnp.bfloat16)
    real_part = visibility[:, :, :, 0].astype(jnp.float32)
    imag_part = visibility[:, :, :, 1].astype(jnp.float32)
    gain_re = gains[:, 0][:, None, None, :]
    gain_im = gains[:, 1][:, None, None, :]
    cal_re = gain_re * real_part - gain_im * imag_part
    cal_im = gain_re * imag_part + gain_im * real_part
    weighted = (scale[:, :, :, None, :] * jnp.stack([cal_re, cal_im], axis=3)).astype(jnp.bfloat16)
    stacked = jnp.concatenate([weighted, weight[:, :, :, None, :]], axis=3)
    taps = spline_taps(fraction)
    tap_index = jnp.arange(4).reshape(1, 1, 1, 4)
    shifts = offsets.reshape(1, local_nights, 1, 1)
    tap_values = taps.reshape(1, local_nights, 1, 4)
    padded_slab = extended(stacked, (("lst", 1),), sample_count)
    out_row = jnp.arange(sample_count).reshape(sample_count, 1, 1, 1)
    source = jnp.arange(3 * sample_count).reshape(1, 1, 3 * sample_count, 1)
    target = out_row - shifts + tap_index - 1 + sample_count
    matrix = jnp.sum(jnp.where(source == target, tap_values, 0.0), axis=-1).astype(jnp.bfloat16)
    partial_numerator = jnp.dot(
        matrix.reshape(sample_count, local_nights * 3 * sample_count),
        padded_slab.reshape(local_nights * 3 * sample_count, baseline_count * 3 * channel_count),
        preferred_element_type=jnp.float32,
    )
    partial_numerator = partial_numerator.reshape(sample_count, baseline_count, 3, channel_count)
    totals = lax.psum(partial_numerator, "night")
    denominator_sum = totals[:, :, 2]
    binned = (
        totals[:, :, 0:2] / (denominator_sum[:, :, None, :] + prior[None, None, None, :])
    ).astype(jnp.bfloat16)
    return (binned, denominator_sum)


def solution(mesh):
    in_specs = (
        P("night", "lst", None, None, None),
        P("night", "lst", None, None),
        P("night", "lst"),
        P("night"),
        P("night"),
        P("night", None, None),
        P("night", None),
        P(),
    )
    out_specs = (P("lst", None, None, None), P("lst", None, None))
    return jax.shard_map(shards, mesh=mesh, in_specs=in_specs, out_specs=out_specs, check_vma=False)
```

profile of v0, /device:TPU:0, one launch (start us, length us, event | category | flops | bytes accessed | tf_op | source)
XLA Modules:
  0.0 172.8 jit_solution(5491326670959882846)
XLA Ops:
  7.2 0.0 copy-start.3
  7.2 0.0 copy-start.1
  7.2 0.0 copy-start.4
  7.2 0.0 all-reduce.2.cloned.1.call-start
  7.2 0.8 slice_reduce_fusion.1
  8.1 3.0 %fusion.11 = (bf16[1,8,16,1,1536]{4,3,2,1,0:T(2,128)(2,1)S(1)}, bf16[1,8,16,1,1536]{4,3,2,1,0:T(2,128)(2,1)S(1)}) fusion(bf16[1,8,16,2,1536]{4,3,2,1,0:T(2,128)(2,1)} %param.8), kind=kLoop, calls=%fused_computation.29 | loop fusion | bytes 1572864 | tf_op jit(solution)/shard_map/slice | solution.py:37
  11.1 0.0 copy-done.3
  11.2 0.0 copy-done.1
  11.2 0.0 copy-done.4
  11.2 0.2 fusion.7
  11.4 0.3 fusion.4
  11.7 0.1 fusion.3
  11.8 0.1 pad_maximum_fusion.1
  11.9 3.9 %collective-permute-start.1 = (bf16[1,8,16,3,1536]{4,2,3,1,0:T(8,128)(2,1)S(1)}, bf16[1,8,16,3,1536]{4,2,3,1,0:T(8,128)(2,1)S(1)}, u32[]{:S(2)}, u32[]{:S(2)}) collective-permute-start(bf16[1,8,16,3,1536]{4,2,3,1,0:T(8,128)(2,1)S(1)} %pad_maximum_fusion.1), channel_id=1, source_target_pairs={{8,0},{16,8},{24,16},{0,24},{9,1},{17,9},{25,17},{1,25},{10,2},{18... | collective-permute-start | bytes 3538952 | tf_op jit(solution)/shard_map/ppermute | solution.py:15
  15.9 0.0 collective-permute-start
  17.2 0.1 maximum_bitcast_fusion
  17.3 0.1 select_reduce_fusion
  17.4 24.9 %collective-permute-done.1 = bf16[1,8,16,3,1536]{4,2,3,1,0:T(8,128)(2,1)S(1)} collective-permute-done((bf16[1,8,16,3,1536]{4,2,3,1,0:T(8,128)(2,1)S(1)}, bf16[1,8,16,3,1536]{4,2,3,1,0:T(8,128)(2,1)S(1)}, u32[]{:S(2)}, u32[]{:S(2)}) %collective-permute-start.1) | collective-permute-done | bytes 1179680 | tf_op jit(solution)/shard_map/ppermute | solution.py:15
  42.3 25.1 %collective-permute-done = bf16[1,8,16,3,1536]{4,2,3,1,0:T(8,128)(2,1)S(1)} collective-permute-done((bf16[1,8,16,3,1536]{4,2,3,1,0:T(8,128)(2,1)S(1)}, bf16[1,8,16,3,1536]{4,2,3,1,0:T(8,128)(2,1)S(1)}, u32[]{:S(2)}, u32[]{:S(2)}) %collective-permute-start) | collective-permute-done | bytes 1179680 | tf_op jit(solution)/shard_map/ppermute | solution.py:14
  67.4 0.4 pad_maximum_fusion
  67.8 5.4 %copy.25 = bf16[1,24,16,3,1536]{4,3,2,1,0:T(4,128)(2,1)} copy(bf16[1,24,16,3,1536]{4,2,3,1,0:T(8,128)(2,1)S(1)} %pad_maximum_fusion) | data formatting | bytes 7077888 | tf_op jit(solution)/shard_map/concatenate | solution.py:16
  73.2 6.2 %reshape.136 = bf16[24,73728]{1,0:T(8,128)(2,1)S(1)} reshape(bf16[1,24,16,3,1536]{4,3,2,1,0:T(4,128)(2,1)} %copy.25) | data formatting | bytes 7077888 | tf_op jit(solution)/shard_map/reshape | solution.py:56
  79.4 6.2 %dot_general.8 = bf16[16,3,1536,24]{2,1,0,3:T(4,128)(2,1)} reshape(bf16[73728,24]{0,1:T(8,128)(2,1)S(1)} %bitcast.25) | data formatting | bytes 7077888 | tf_op jit(solution)/shard_map/dot_general | solution.py:54
  85.6 8.3 %fusion = f32[8,16,3,1536]{3,0,2,1:T(8,128)} fusion(bf16[16,3,1536,24]{2,1,0,3:T(4,128)(2,1)} %dot_general.8, bf16[8,24]{1,0:T(8,128)(2,1)S(1)} %select_reduce_fusion), kind=kOutput, calls=%fused_computation.1 | convolution fusion | flops 28311552 | bytes 5898624 | tf_op jit(solution)/shard_map/dot_general | solution.py:54
  93.8 0.0 copy-start.2
  93.8 0.0 all-reduce.2.cloned.1.call-update
  93.9 67.2 %all-reduce.2.cloned.1.call-done = f32[8,16,3,1536]{3,0,2,1:T(8,128)} async-done(((f32[8,16,3,1536]{3,0,2,1:T(8,128)}), f32[8,16,3,1536]{3,0,2,1:T(8,128)}) %all-reduce.2.cloned.1.call-update) | async-done | bytes 2359312 | tf_op jit(solution)/shard_map/psum | solution.py:60
  161.0 0.0 copy-done.2
  161.0 0.0 copy-start
  161.0 1.4 slice_bitcast_fusion
  162.5 0.4 copy-done
  162.9 0.2 fusion.2
  163.1 1.5 copy.27
  164.6 1.3 copy.28
  (3 shorter events, 0.0 us)
Async XLA Ops:
  7.2 4.0 %copy-start.3 = (f32[1,1536]{1,0:T(1,128)S(1)}, f32[1,1536]{1,0:T(1,128)}, u32[]{:S(2)}) copy-start(f32[1,1536]{1,0:T(1,128)} %param.14) | copy-start | bytes 18436
  7.2 4.0 %copy-start.1 = (s32[1,8,16,1536]{3,2,1,0:T(8,128)S(1)}, s32[1,8,16,1536]{3,2,1,0:T(8,128)}, u32[]{:S(2)}) copy-start(s32[1,8,16,1536]{3,2,1,0:T(8,128)} %param.9) | copy-start | bytes 2359300
  7.2 4.0 %copy-start.4 = (s32[1,8]{1,0:T(1,128)S(1)}, s32[1,8]{1,0:T(1,128)}, u32[]{:S(2)}) copy-start(s32[1,8]{1,0:T(1,128)} %param.10) | copy-start | bytes 100
  7.2 153.8 %all-reduce.2.cloned.1.call-start = ((), (), s32[]{:S(2)}) async-start(), calls=%async_computation | async-start | bytes 4718592 | tf_op jit(solution)/shard_map/psum | solution.py:60
  11.9 30.3 %collective-permute-start.1 = (bf16[1,8,16,3,1536]{4,2,3,1,0:T(8,128)(2,1)S(1)}, bf16[1,8,16,3,1536]{4,2,3,1,0:T(8,128)(2,1)S(1)}, u32[]{:S(2)}, u32[]{:S(2)}) collective-permute-start(bf16[1,8,16,3,1536]{4,2,3,1,0:T(8,128)(2,1)S(1)} %pad_maximum_fusion.1), channel_id=1, source_target_pairs={{8,0},{16,8},{24,16},{0,24},{9,1},{17,9},{25,17},{1,25},{10,2},{18... | collective-permute-start | bytes 3538952 | tf_op jit(solution)/shard_map/ppermute | solution.py:15
  15.9 51.5 %collective-permute-start = (bf16[1,8,16,3,1536]{4,2,3,1,0:T(8,128)(2,1)S(1)}, bf16[1,8,16,3,1536]{4,2,3,1,0:T(8,128)(2,1)S(1)}, u32[]{:S(2)}, u32[]{:S(2)}) collective-permute-start(bf16[1,8,16,3,1536]{4,2,3,1,0:T(8,128)(2,1)S(1)} %pad_maximum_fusion.1), channel_id=1, source_target_pairs={{0,8},{8,16},{16,24},{24,0},{1,9},{9,17},{17,25},{25,1},{2,10},{10... | collective-permute-start | bytes 3538952 | tf_op jit(solution)/shard_map/ppermute | solution.py:14
  93.8 67.2 %copy-start.2 = (f32[1536]{0:T(1024)S(1)}, f32[1536]{0:T(1024)}, u32[]{:S(2)}) copy-start(f32[1536]{0:T(1024)} %param.15) | copy-start | bytes 18436
  161.0 1.9 %copy-start = (f32[8,16,3,1536]{3,0,2,1:T(8,128)S(1)}, f32[8,16,3,1536]{3,0,2,1:T(8,128)}, u32[]{:S(2)}) copy-start(f32[8,16,3,1536]{3,0,2,1:T(8,128)} %all-reduce.2.cloned.1.call-done) | copy-start | bytes 7077892
Sparse Core Ops, SparseCore 0:
  94.0 67.0 all-reduce.1
where the time goes:
time: 173 us
  waiting for transfers between devices  117 us (68%)
  local copies, waits for them, and re-layouts  24.9 us (14%)
  between operations  15.5 us (9%)
  matrix products  8.26 us (5%)
  starting transfers between devices  3.99 us (2%)
  other arithmetic  2.95 us (2%)
    psum x1, waiting for transfers between devices, shards(): totals = lax.psum(partial_numerator, 'night')  67.2 us
    ppermute x1, waiting for transfers between devices, extended(): before = lax.ppermute(last, axis, up)  25.1 us
    ppermute x1, waiting for transfers between devices, extended(): after = lax.ppermute(first, axis, down)  24.9 us
    dot_general x1, matrix products, shards(): jnp.dot(matrix.reshape(sample_count, local_nights * 3 * sample_count), pa...  8.26 us
    dot_general x1, local copies, waits for them, and re-layouts, shards(): jnp.dot(matrix.reshape(sample_count, local_nights * 3 * sample_count), pa...  6.2 us
    reshape x1, local copies, waits for them, and re-layouts, shards(): padded_slab.reshape(local_nights * 3 * sample_count, baseline_count * 3 *...  6.2 us
    concatenate x1, local copies, waits for them, and re-layouts, extended(): x = jnp.concatenate([before, x, after], axis=dim)  5.36 us
    ppermute x1, starting transfers between devices, extended(): after = lax.ppermute(first, axis, down)  3.95 us
  transfers between devices with their start and end apart: 3, of which 3 were waited for; matrix products, arithmetic and copies ran while one was open for 0% of the time, Pallas kernels for 0%

commit v1 on v0

--- a/solution.py
+++ b/solution.py
@@ -57,7 +57,7 @@
         preferred_element_type=jnp.float32,
     )
     partial_numerator = partial_numerator.reshape(sample_count, baseline_count, 3, channel_count)
-    totals = lax.psum(partial_numerator, "night")
+    totals = lax.all_gather(partial_numerator, "night").sum(axis=0)
     denominator_sum = totals[:, :, 2]
     binned = (
         totals[:, :, 0:2] / (denominator_sum[:, :, None, :] + prior[None, None, None, :])

time: 173 us -> 282 us (1.63)
  waiting for transfers between devices: 117 us -> 219 us
  other arithmetic: 2.95 us -> 10.7 us
    all_gather x0 -> x1, waiting for transfers between devices: none -> 169 us  [shards(): totals = lax.all_gather(partial_numerator, 'night').sum(axis=0)]
    psum x1 -> x0, waiting for transfers between devices: 67.2 us -> none  [shards(): totals = lax.psum(partial_numerator, 'night')]
    reduce_sum x0 -> x1, other arithmetic: none -> 8.94 us  [shards(): totals = lax.all_gather(partial_numerator, 'night').sum(axis=0)]
where the time goes in v1:
time: 282 us
  waiting for transfers between devices  219 us (78%)
  local copies, waits for them, and re-layouts  24.4 us (9%)
  between operations  15.5 us (5%)
  other arithmetic  10.7 us (4%)
  matrix products  8.22 us (3%)
  starting transfers between devices  3.99 us (1%)
    all_gather x1, waiting for transfers between devices, shards(): totals = lax.all_gather(partial_numerator, 'night').sum(axis=0)  169 us
    ppermute x1, waiting for transfers between devices, extended(): before = lax.ppermute(last, axis, up)  25.1 us
    ppermute x1, waiting for transfers between devices, extended(): after = lax.ppermute(first, axis, down)  24.9 us
    reduce_sum x1, other arithmetic, shards(): totals = lax.all_gather(partial_numerator, 'night').sum(axis=0)  8.94 us
    dot_general x1, matrix products, shards(): jnp.dot(matrix.reshape(sample_count, local_nights * 3 * sample_count), pa...  8.22 us
    reshape x1, local copies, waits for them, and re-layouts, shards(): padded_slab.reshape(local_nights * 3 * sample_count, baseline_count * 3 *...  6.2 us
    dot_general x1, local copies, waits for them, and re-layouts, shards(): jnp.dot(matrix.reshape(sample_count, local_nights * 3 * sample_count), pa...  6.18 us
  transfers between devices with their start and end apart: 3, of which 3 were waited for; matrix products, arithmetic and copies ran while one was open for 0% of the time, Pallas kernels for 0%

profile of v1, /device:TPU:0, one launch (start us, length us, event | category | flops | bytes accessed | tf_op | source)
XLA Modules:
  0.0 281.6 jit_solution(8261686402865041481)
XLA Ops:
  7.2 0.0 copy-start.2
  7.2 0.0 copy-start.3
  7.2 0.0 copy-start
  7.2 0.0 all-gather.3.cloned.1.call-start
  7.2 0.8 slice_reduce_fusion.1
  8.1 3.0 %fusion.11 = (bf16[1,8,16,1,1536]{4,3,2,1,0:T(2,128)(2,1)S(1)}, bf16[1,8,16,1,1536]{4,3,2,1,0:T(2,128)(2,1)S(1)}) fusion(bf16[1,8,16,2,1536]{4,3,2,1,0:T(2,128)(2,1)} %param.8), kind=kLoop, calls=%fused_computation.30 | loop fusion | bytes 1572864 | tf_op jit(solution)/shard_map/slice | solution.py:37
  11.1 0.0 copy-done.2
  11.1 0.0 copy-done.3
  11.1 0.0 copy-done
  11.1 0.2 fusion.7
  11.3 0.3 fusion.4
  11.6 0.1 fusion.3
  11.8 0.1 pad_maximum_fusion.1
  11.9 3.9 %collective-permute-start.1 = (bf16[1,8,16,3,1536]{4,2,3,1,0:T(8,128)(2,1)S(1)}, bf16[1,8,16,3,1536]{4,2,3,1,0:T(8,128)(2,1)S(1)}, u32[]{:S(2)}, u32[]{:S(2)}) collective-permute-start(bf16[1,8,16,3,1536]{4,2,3,1,0:T(8,128)(2,1)S(1)} %pad_maximum_fusion.1), channel_id=1, source_target_pairs={{8,0},{16,8},{24,16},{0,24},{9,1},{17,9},{25,17},{1,25},{10,2},{18... | collective-permute-start | bytes 3538952 | tf_op jit(solution)/shard_map/ppermute | solution.py:15
  15.9 0.0 collective-permute-start
  17.2 0.1 maximum_bitcast_fusion
  17.3 0.1 select_reduce_fusion
  17.4 24.9 %collective-permute-done.1 = bf16[1,8,16,3,1536]{4,2,3,1,0:T(8,128)(2,1)S(1)} collective-permute-done((bf16[1,8,16,3,1536]{4,2,3,1,0:T(8,128)(2,1)S(1)}, bf16[1,8,16,3,1536]{4,2,3,1,0:T(8,128)(2,1)S(1)}, u32[]{:S(2)}, u32[]{:S(2)}) %collective-permute-start.1) | collective-permute-done | bytes 1179680 | tf_op jit(solution)/shard_map/ppermute | solution.py:15
  42.2 25.1 %collective-permute-done = bf16[1,8,16,3,1536]{4,2,3,1,0:T(8,128)(2,1)S(1)} collective-permute-done((bf16[1,8,16,3,1536]{4,2,3,1,0:T(8,128)(2,1)S(1)}, bf16[1,8,16,3,1536]{4,2,3,1,0:T(8,128)(2,1)S(1)}, u32[]{:S(2)}, u32[]{:S(2)}) %collective-permute-start) | collective-permute-done | bytes 1179680 | tf_op jit(solution)/shard_map/ppermute | solution.py:14
  67.3 0.4 pad_maximum_fusion
  67.8 5.4 %copy.23 = bf16[1,24,16,3,1536]{4,3,2,1,0:T(4,128)(2,1)} copy(bf16[1,24,16,3,1536]{4,2,3,1,0:T(8,128)(2,1)S(1)} %pad_maximum_fusion) | data formatting | bytes 7077888 | tf_op jit(solution)/shard_map/concatenate | solution.py:16
  73.1 6.2 %reshape.140 = bf16[24,73728]{1,0:T(8,128)(2,1)S(1)} reshape(bf16[1,24,16,3,1536]{4,3,2,1,0:T(4,128)(2,1)} %copy.23) | data formatting | bytes 7077888 | tf_op jit(solution)/shard_map/reshape | solution.py:56
  79.3 6.2 %dot_general.10 = bf16[16,3,1536,24]{2,1,0,3:T(4,128)(2,1)} reshape(bf16[73728,24]{0,1:T(8,128)(2,1)S(1)} %bitcast.27) | data formatting | bytes 7077888 | tf_op jit(solution)/shard_map/dot_general | solution.py:54
  85.5 8.2 %fusion = f32[8,16,3,1536]{3,0,2,1:T(8,128)} fusion(bf16[16,3,1536,24]{2,1,0,3:T(4,128)(2,1)} %dot_general.10, bf16[8,24]{1,0:T(8,128)(2,1)S(1)} %select_reduce_fusion), kind=kOutput, calls=%fused_computation.2 | convolution fusion | flops 28311552 | bytes 5898624 | tf_op jit(solution)/shard_map/dot_general | solution.py:54
  93.7 0.0 all-gather.3.cloned.1.call-update
  93.8 0.0 copy-start.1
  93.8 168.7 %all-gather.3.cloned.1.call-done = f32[64,16,3,1536]{3,0,2,1:T(8,128)} async-done(((f32[8,16,3,1536]{3,0,2,1:T(8,128)}), f32[64,16,3,1536]{3,0,2,1:T(8,128)}) %all-gather.3.cloned.1.call-update) | async-done | bytes 18874384 | tf_op jit(solution)/shard_map/all_gather | solution.py:60
  262.5 8.9 %bitcast_reduce_fusion = f32[8,16,3,1536]{3,0,2,1:T(8,128)S(1)} fusion(f32[64,16,3,1536]{3,0,2,1:T(8,128)} %all-gather.3.cloned.1.call-done), kind=kLoop, calls=%fused_computation | loop fusion | flops 4128768 | bytes 21233664 | tf_op jit(solution)/shard_map/reduce_sum | solution.py:60
  271.5 0.0 copy-done.1
  271.5 0.2 slice_bitcast_fusion
  271.7 0.2 fusion.2
  271.9 1.3 copy.26
  273.2 1.5 copy.25
  (3 shorter events, 0.0 us)
Async XLA Ops:
  7.2 3.9 %copy-start.2 = (f32[1,1536]{1,0:T(1,128)S(1)}, f32[1,1536]{1,0:T(1,128)}, u32[]{:S(2)}) copy-start(f32[1,1536]{1,0:T(1,128)} %param.14) | copy-start | bytes 18436
  7.2 4.0 %copy-start.3 = (s32[1,8]{1,0:T(1,128)S(1)}, s32[1,8]{1,0:T(1,128)}, u32[]{:S(2)}) copy-start(s32[1,8]{1,0:T(1,128)} %param.10) | copy-start | bytes 100
  7.2 4.0 %copy-start = (s32[1,8,16,1536]{3,2,1,0:T(8,128)S(1)}, s32[1,8,16,1536]{3,2,1,0:T(8,128)}, u32[]{:S(2)}) copy-start(s32[1,8,16,1536]{3,2,1,0:T(8,128)} %param.9) | copy-start | bytes 2359300
  7.2 255.3 %all-gather.3.cloned.1.call-start = ((), (), s32[]{:S(2)}) async-start(), calls=%async_computation | async-start | bytes 21233664 | tf_op jit(solution)/shard_map/all_gather | solution.py:60
  11.9 30.3 %collective-permute-start.1 = (bf16[1,8,16,3,1536]{4,2,3,1,0:T(8,128)(2,1)S(1)}, bf16[1,8,16,3,1536]{4,2,3,1,0:T(8,128)(2,1)S(1)}, u32[]{:S(2)}, u32[]{:S(2)}) collective-permute-start(bf16[1,8,16,3,1536]{4,2,3,1,0:T(8,128)(2,1)S(1)} %pad_maximum_fusion.1), channel_id=1, source_target_pairs={{8,0},{16,8},{24,16},{0,24},{9,1},{17,9},{25,17},{1,25},{10,2},{18... | collective-permute-start | bytes 3538952 | tf_op jit(solution)/shard_map/ppermute | solution.py:15
  15.9 51.5 %collective-permute-start = (bf16[1,8,16,3,1536]{4,2,3,1,0:T(8,128)(2,1)S(1)}, bf16[1,8,16,3,1536]{4,2,3,1,0:T(8,128)(2,1)S(1)}, u32[]{:S(2)}, u32[]{:S(2)}) collective-permute-start(bf16[1,8,16,3,1536]{4,2,3,1,0:T(8,128)(2,1)S(1)} %pad_maximum_fusion.1), channel_id=1, source_target_pairs={{0,8},{8,16},{16,24},{24,0},{1,9},{9,17},{17,25},{25,1},{2,10},{10... | collective-permute-start | bytes 3538952 | tf_op jit(solution)/shard_map/ppermute | solution.py:14
  93.8 177.7 %copy-start.1 = (f32[1536]{0:T(1024)S(1)}, f32[1536]{0:T(1024)}, u32[]{:S(2)}) copy-start(f32[1536]{0:T(1024)} %param.15) | copy-start | bytes 18436
Sparse Core Ops, SparseCore 0:
  93.9 168.5 all-gather.2
